TPU v7x, 256 devices: a whole 4x4x8 slice. The times are simulated.
256 devices in a mesh: box: 16 (over x, y), row: 16 (over z, core).
Axes of the slice: x: 4, y: 4, z: 8, core: 2. Of those that a mesh axis runs over, the one named last changes fastest.
Arguments:
- child_maps: float32 [2, 32, 1024, 1024], P(None, 'box', 'row'), may hold values from -1 to 1
- child_faces: int32 [32, 1024], replicated, may hold values from -1 to 511, as said below
- parent_faces: int32 [16, 1024], replicated, may hold values from -1 to 511, as said below
Outputs:
- parent_maps: float32 [2, 16, 1024, 1024], P(None, 'box', 'row')
- grand_maps: float32 [2, 1024, 8192], P(None, 'row', 'box')
Inputs may be any that keep to these rules, and one draw needn't show every extreme that they name: `child_faces`: in each row, every face position 0 to 511 occurs exactly once, and each aligned block of 32 nodes holds exactly 16 shared nodes. `parent_faces`: in each row, every face position 0 to 511 occurs exactly once, and each aligned block of 32 nodes holds exactly 16 shared nodes.
All inputs are finite; a program needn't handle non-finite values.
Results may differ from a plain program's by a relative error of at most 0.00012.
Values sent between devices are 32-bit elements; how exact they have to be, the bound alone decides.
A program may use at most 128 MiB of HBM per device.

v0:
```python
import functools

import jax
import jax.numpy as jnp
from jax import lax
from jax.experimental import pallas as pl
from jax.experimental.pallas import tpu as pltpu
from jax.sharding import PartitionSpec as P

MESH = pl.DeviceIdType.MESH
F32 = jnp.float32
BF16 = jnp.bfloat16
ORDER = 1024
SHARED = 512
RING = 16
TOTAL = 192
DEPTHS = (4, 4)


def order_parent(ssm, sso, sxm, sxo):
    return [
        (ssm, 0), (sxm, 0), (sso, 0), (ssm, 1), (sso, 1), (sxo, 0), (ssm, 2), (sso, 2),
        (sxm, 1), (ssm, 3), (sso, 3), (sxo, 1), (sxm, 2), (sxo, 2), (sxm, 3), (sxo, 3),
    ]


def order_grand(ssi, ssr, sso, sxm, sxo):
    return [
        (ssi, 0), (ssr, 0), (sxm, 0), (sso, 0), (ssi, 1), (ssr, 1), (sso, 1), (ssi, 2), (ssr, 2),
        (sxm, 1), (sso, 2), (ssi, 3), (ssr, 3), (sxo, 0), (sso, 3), (sxm, 2), (sxo, 1), (sxm, 3),
        (sxo, 2), (sxo, 3),
    ]


def dot(a, b):
    return jnp.dot(a, b, preferred_element_type=F32)


def dot_nt(a, b):
    return lax.dot_general(a, b, (((1,), (1,)), ((), ())), preferred_element_type=F32)


def split(x):
    hi = x.astype(BF16)
    return hi, (x - hi.astype(F32)).astype(BF16)


def iota(shape, dim):
    return lax.broadcasted_iota(jnp.int32, shape, dim)


def one_hot(mask):
    return jnp.where(mask, 1.0, 0.0).astype(BF16)


def prefix_counts(rows):
    width = rows.shape[1]
    lower = one_hot(iota((width, width), 0) < iota((width, width), 1))
    return dot(jnp.where(rows < 0, 1.0, 0.0).astype(BF16), lower).astype(jnp.int32)


def chunked(faces):
    return jnp.concatenate([faces[:, 256 * t : 256 * t + 256] for t in range(4)], axis=0)


def build_selectors(own, other, local, face_ref, outer_ref):
    rows = jnp.concatenate([chunked(own), chunked(other)], axis=0)
    counts = prefix_counts(rows)
    lane = iota((1, 256), 1)
    slot = iota((128, 256), 0)
    own_value = own.astype(F32)
    for t in range(4):
        outer_rank = jnp.where(rows[t : t + 1] < 0, counts[t : t + 1], -1)
        outer_ref[t] = one_hot(outer_rank == slot)
        face_row = rows[4 + t : 5 + t]
        shared_rank = jnp.where(face_row < 0, -1, lane - counts[4 + t : 5 + t])
        wanted = jnp.sum(
            jnp.where(shared_rank == slot, face_row.astype(F32), 0.0), axis=1, keepdims=True
        )
        face_ref[128 * t : 128 * t + 128, :] = one_hot(own_value == wanted)
    count = prefix_counts(jnp.broadcast_to(local, (8, 64)))[0:1]
    target = jnp.where(local < 0, 32 + count, iota((1, 64), 1) - count)
    return one_hot(target == iota((64, 64), 0))


def select(parts, row_hot, face_ref, outer_ref):
    stack = []
    for value in parts:
        for piece in split(value):
            stack.append(dot(row_hot, piece).astype(BF16))
    stack = jnp.concatenate(stack, axis=0)
    face = dot_nt(stack, face_ref[...])
    outer = jnp.concatenate(
        [dot_nt(stack[:, 256 * t : 256 * t + 256], outer_ref[t]) for t in range(4)], axis=1
    )
    face = [face[0:64] + face[64:128], face[128:192] + face[192:256]]
    outer = [outer[0:64] + outer[64:128], outer[128:192] + outer[192:256]]
    return face, outer


def complex_product(x, w):
    m = x[0].shape[0]
    hi, lo = split(jnp.concatenate(x, axis=0))
    both = jnp.concatenate([hi, lo], axis=0)
    sums = []
    for part in range(2):
        main = dot(both, w[0, part])
        sums.append(main[: 2 * m] + main[2 * m :] + dot(hi, w[1, part]))
    by_real, by_imag = sums
    return [by_real[:m] - by_imag[m:], by_imag[:m] + by_real[m:]]


def convert(gathered, pieces, role):
    @pl.loop(0, RING)
    def _(k):
        rows = pl.ds(pl.multiple_of(k * 32, 32), 32)
        for part in range(2):
            hi, lo = split(gathered[role, k, part])
            pieces[role, 0, part, rows, :] = hi
            pieces[role, 1, part, rows, :] = lo


def weave(alpha, beta):
    return jnp.concatenate([alpha[0:16], beta[0:16], alpha[16:32], beta[16:32]], axis=0)


def kernel(
    maps_ref, child_faces_ref, parent_faces_ref, parent_out, grand_ref,
    maps, child_rows, parent_rows, parent_ref,
    ss1, sx1, xs1, xx1, ss2, sx2, xs2, xx2, out_ss, out_sx, out_xs, out_xx, out_sx2, out_xx2,
    face_hot, outer_hot, face_hot2, outer_hot2, wss, wsx, wsx2, send, recv, local_sem,
):
    box, row = lax.axis_index("box"), lax.axis_index("row")
    par = lax.rem(box, 2)
    mate = box + 1 - 2 * par
    core = lax.rem(row, 2)
    z = lax.div(row, 2)
    sib = row + 1 - 2 * core
    up, down = lax.rem(row + 2, RING), lax.rem(row + RING - 2, RING)
    to_up, to_down, to_sib, to_mate = (box, up), (box, down), (box, sib), (mate, row)

    barrier = pltpu.get_barrier_semaphore()
    for target in (to_up, to_down, to_sib, to_mate):
        pl.semaphore_signal(barrier, inc=1, device_id=target, device_id_type=MESH)

    first = 2 * (box - par)

    def group(i):
        return pl.ds(pl.multiple_of(8 * lax.div(i, 8), 8), 8)

    loads = [
        pltpu.make_async_copy(child_faces_ref.at[group(first)], child_rows, local_sem.at[0]),
        pltpu.make_async_copy(maps_ref.at[:, 1 - par], maps.at[1], local_sem.at[1]),
        pltpu.make_async_copy(maps_ref.at[:, par], maps.at[0], local_sem.at[2]),
        pltpu.make_async_copy(parent_faces_ref.at[group(box)], parent_rows, local_sem.at[3]),
    ]
    for c in loads:
        c.start()

    ids = {}
    pending = []

    def copy(src, dst, target, key):
        k = ids.setdefault(key, len(ids))
        return pltpu.make_async_remote_copy(
            src_ref=src, dst_ref=dst, send_sem=send.at[k], recv_sem=recv.at[k],
            device_id=target, device_id_type=MESH,
        )

    def push(src, dst, target, key):
        c = copy(src, dst, target, key)
        c.start()
        pending.append(c)

    def arrived(dst, key):
        copy(dst, dst, to_mate, key).wait_recv()

    def away(base, way, hops):
        return lax.rem(base + 2 * RING + (2 if way else -2) * hops, RING)

    class Section:
        def __init__(self, name, buf, role, part=None, forward=False, source=None):
            self.name, self.buf, self.role = name, buf, role
            self.part, self.forward, self.source = part, forward, source

        def block(self, slot):
            whole = self.buf.at[self.role, slot]
            return whole if self.part is None else whole.at[self.part]

        def piece(self, base, way, hop):
            slot = away(base, way, hop)
            if hop < 3:
                return self.block(slot)
            if self.part is not None:
                return self.buf.at[self.role, slot, self.part, pl.ds(16 * way, 16)]
            return self.buf.at[self.role, slot, way]

        def to_mate(self, slot, what):
            if self.forward:
                block = self.block(slot)
                push(block, block, to_mate, (self.name, "mate", what))

        def send(self, way, hop):
            if hop == 0 and way == 0 and self.source is not None:
                arrived(self.block(row), self.source)
            piece = self.piece(row, way, hop)
            push(piece, piece, to_down if way else to_up, (self.name, way, hop))
            if hop == 0 and way == 1:
                own = self.block(row)
                push(own, own, to_sib, (self.name, "sib", "own"))
                self.to_mate(row, "own")

        def receive(self, way, hop):
            slot = away(row, way, hop + 1)
            if hop < 3:
                piece = self.block(slot)
            else:
                piece = self.piece(away(row, way, 1), way, hop)
            arrived(piece, (self.name, way, hop))
            return slot, piece

        def share(self, way, hop, slot, piece):
            push(piece, piece, to_sib, (self.name, "sib", way, hop))
            if hop < 3:
                self.to_mate(slot, (way, hop))
            elif way == 1:
                self.to_mate(slot, "far")

        def done(self):
            arrived(self.block(sib), (self.name, "sib", "own"))
            for way in range(2):
                for hop in range(3):
                    arrived(self.block(away(sib, way, hop + 1)), (self.name, "sib", way, hop))
                arrived(self.piece(away(sib, way, 1), way, 3), (self.name, "sib", way, 3))

    class Flow:
        def __init__(self, order, depth):
            self.order, self.depth = order, depth
            self.sent = self.got = 0

        def ready(self, got):
            more = []
            while self.sent < len(self.order) and self.sent < got + self.depth:
                section, hop = self.order[self.sent]
                if hop and (section, hop - 1) not in self.order[:got]:
                    break
                more.append((section, hop))
                self.sent += 1
            return more

        def begin(self):
            for section, hop in self.ready(0):
                for way in range(2):
                    section.send(way, hop)

        def advance(self, upto=None):
            upto = self.got + 1 if upto is None else upto
            while self.got < min(upto, len(self.order)):
                section, hop = self.order[self.got]
                following = self.ready(self.got + 1)
                for way in range(2):
                    slot, piece = section.receive(way, hop)
                    for later, later_hop in following:
                        later.send(way, later_hop)
                    section.share(way, hop, slot, piece)
                self.got += 1

        def through(self, section):
            return self.order.index((section, 3)) + 1

    class Mirror:
        def __init__(self, name, mine, buf, role):
            self.name, self.mine, self.buf, self.role = name, mine, buf, role

        def block(self, slot):
            return self.buf.at[self.role, slot, 1]

        def take(self, slot, what):
            block = self.block(slot)
            arrived(block, (self.mine, "mate", what))
            push(block, block, to_sib, (self.name, "sib", what))

        def start(self):
            self.take(row, "own")

        def step(self, j):
            for way in range(2):
                self.take(away(row, way, j + 1), (way, j))

        def last(self):
            self.take(away(row, 0, 4), "far")

        def done(self):
            arrived(self.block(sib), (self.name, "sib", "own"))
            for way in range(2):
                for j in range(3):
                    arrived(self.block(away(sib, way, j + 1)), (self.name, "sib", (way, j)))
            arrived(self.block(away(sib, 0, 4)), (self.name, "sib", "far"))

    def faces_of(rows, i):
        inside = lax.rem(i, 8)
        lanes = pl.ds(pl.multiple_of(z * 128, 128), 128)
        whole = jnp.sum(
            jnp.where(iota((8, ORDER), 0) == inside, rows[...], 0), axis=0, keepdims=True
        )
        chunk = jnp.sum(
            jnp.where(iota((8, 128), 0) == inside, rows[:, lanes], 0), axis=0, keepdims=True
        )
        local = jnp.where(core == 0, chunk[:, :64], chunk[:, 64:])
        return whole, local

    loads[0].wait()
    own_faces, local = faces_of(child_rows, first + 1 + par)
    paired, _ = faces_of(child_rows, first + 3 - 3 * par)
    hot = build_selectors(own_faces, paired, local, face_hot, outer_hot)
    loads[1].wait()
    face, outer = select([maps[1, part] for part in range(2)], hot, face_hot, outer_hot)
    for part in range(2):
        out_ss[part] = face[part][:32]
        out_xs[part] = face[part][32:]
        out_sx[part] = outer[part][:32]
        out_xx[part] = outer[part][32:]
    pl.semaphore_wait(barrier, 4)
    push(out_ss, ss1.at[par, row], to_mate, "ss1")

    own_faces, local = faces_of(child_rows, first + 3 * par)
    paired, _ = faces_of(child_rows, first + 2 - par)
    hot = build_selectors(own_faces, paired, local, face_hot, outer_hot)
    loads[2].wait()
    face, outer = select([maps[0, part] for part in range(2)], hot, face_hot, outer_hot)
    for part in range(2):
        ss1[par, row, part] = face[part][:32]
        xs1[par, part] = face[part][32:]
        sx1[par, row, part] = outer[part][:32]
        xx1[par, part] = outer[part][32:]

    def multiply(ss_mine, ss_other, sx_mine, sx_other, xs, xx, wx, emit, flow):
        more = flow.advance
        convert(ss_mine.buf, wss, 1)
        u = [xs[0, part] for part in range(2)]
        lead = complex_product(u, wss.at[1])
        base = [jnp.concatenate([lead[part], -xs[1, part]], axis=0) for part in range(2)]
        more()
        convert(ss_mine.buf, wss, 0)
        w = base
        for term in range(3):
            t = complex_product(w, wss.at[0])
            more()
            t = complex_product(t, wss.at[1])
            w = [base[part] + t[part] for part in range(2)]
            more()
        t = complex_product(w, wss.at[0])
        t = [jnp.concatenate([t[part][:32] + u[part], t[part][32:]], axis=0) for part in range(2)]
        more(flow.through(sx_mine))
        sx_mine.done()
        convert(sx_mine.buf, wx, par)
        mine = complex_product([jnp.where(par == 0, w[p], t[p]) for p in range(2)], wx.at[par])
        more(flow.through(sx_other))
        sx_other.done()
        convert(sx_mine.buf, wx, 1 - par)
        other = complex_product([jnp.where(par == 0, t[p], w[p]) for p in range(2)], wx.at[1 - par])
        alpha = [jnp.where(par == 0, mine[p], other[p]) for p in range(2)]
        beta = [jnp.where(par == 0, other[p], mine[p]) for p in range(2)]
        width = alpha[0].shape[1]
        stack = []
        for part in range(2):
            left = weave(xx[0, part] + alpha[part][:32], alpha[part][32:])
            right = weave(-beta[part][:32], xx[1, part] - beta[part][32:])
            stack.append((left, right))
        rank, place = iota((256, 256), 0), iota((256, 256), 1)
        inside = jnp.where(rank < 128, rank, rank - 128)
        spot = 32 * lax.div(inside, 16) + lax.rem(inside, 16) + jnp.where(rank < 128, 0, 16)
        place_hot = one_hot(spot == place)
        for tile in range(width // 128):
            cols = slice(128 * tile, 128 * tile + 128)
            packed = jnp.concatenate(
                [
                    jnp.concatenate([stack[part][0][:, cols], stack[part][1][:, cols]], axis=1)
                    for part in range(2)
                ],
                axis=0,
            )
            hi, lo = split(packed)
            spread = dot(jnp.concatenate([hi, lo], axis=0), place_hot)
            spread = spread[:128] + spread[128:]
            for part in range(2):
                emit(part, tile, spread[64 * part : 64 * part + 64])

    def emit_parent(part, tile, value):
        parent_ref[part, :, 256 * tile : 256 * tile + 256] = value

    def emit_grand(part, tile, value):
        grand_ref[part, :, 256 * tile : 256 * tile + 256] = value

    ssm, sso = Section("ssm1", ss1, par), Section("sso1", ss1, 1 - par, source="ss1")
    sxm, sxo = Section("sxm1", sx1, par), Section("sxo1", sx1, 1 - par, source="sx1")
    flow = Flow(order_parent(ssm, sso, sxm, sxo), DEPTHS[0])
    flow.begin()
    loads[3].wait()
    own, loc = faces_of(parent_rows, box)
    pair, _ = faces_of(parent_rows, mate)
    hot2 = build_selectors(own, pair, loc, face_hot2, outer_hot2)
    flow.advance(1)
    push(out_sx, sx1.at[par, row], to_mate, "sx1")
    flow.advance(3)
    push(out_xs, xs1.at[par], to_mate, "xs1")
    push(out_xx, xx1.at[par], to_mate, "xx1")
    flow.advance(max(flow.through(ssm), flow.through(sso)))
    arrived(xs1.at[1 - par], "xs1")
    arrived(xx1.at[1 - par], "xx1")
    ssm.done()
    sso.done()
    multiply(ssm, sso, sxm, sxo, xs1, xx1, wsx, emit_parent, flow)

    face, outer = select([parent_ref[part] for part in range(2)], hot2, face_hot2, outer_hot2)
    for part in range(2):
        ss2[par, row, part] = face[part][:32]
        xs2[par, part] = face[part][32:]
    real = ss2.at[par, row, 0]
    push(real, real, to_mate, "ss2")
    ssi, ssr = Section("ssi2", ss2, par, part=1, forward=True), Section("ssr2", ss2, par, part=0)
    sso = Section("sso2", ss2, 1 - par, part=0, source="ss2")
    mirror = Mirror("mir2", "ssi2", ss2, 1 - par)
    sxm, sxo = Section("sxm2", sx2, par), Section("sxo2", sx2, 1 - par, source="sx2")
    for part in range(2):
        halves = [outer[part][:, :256], outer[part][:, 256:]]
        mine = jnp.where(par == 0, halves[0], halves[1])
        theirs = jnp.where(par == 0, halves[1], halves[0])
        sx2[par, row, part] = mine[:32]
        xx2[par, part] = mine[32:]
        out_sx2[part] = theirs[:32]
        out_xx2[part] = theirs[32:]
    push(out_sx2, sx2.at[par, row], to_mate, "sx2")
    flow = Flow(order_grand(ssi, ssr, sso, sxm, sxo), DEPTHS[1])
    flow.begin()
    store = pltpu.make_async_copy(parent_ref, parent_out.at[:, 0], local_sem.at[4])
    store.start()
    at = [flow.order.index((ssi, hop)) + 1 for hop in range(4)]
    flow.advance(at[0])
    push(xs2.at[par], xs2.at[par], to_mate, "xs2")
    mirror.start()
    flow.advance(at[1])
    mirror.step(0)
    push(out_xx2, xx2.at[par], to_mate, "xx2")
    flow.advance(at[2])
    mirror.step(1)
    flow.advance(max(flow.through(ssi), flow.through(ssr), flow.through(sso)))
    mirror.step(2)
    mirror.last()
    arrived(xs2.at[1 - par], "xs2")
    arrived(xx2.at[1 - par], "xx2")
    ssi.done()
    ssr.done()
    sso.done()
    mirror.done()
    multiply(ssi, sso, sxm, sxo, xs2, xx2, wsx2, emit_grand, flow)

    store.wait()
    for c in pending:
        c.wait_send()


def per_device(child_maps, child_faces, parent_faces):
    def vmem(*shape, dtype=F32):
        return pltpu.VMEM(shape, dtype)

    whole = pl.BlockSpec(memory_space=pltpu.VMEM)
    placed = pl.BlockSpec(memory_space=pltpu.HBM)
    return pl.pallas_call(
        kernel,
        out_shape=(
            jax.ShapeDtypeStruct((2, 1, 64, ORDER), F32),
            jax.ShapeDtypeStruct((2, 64, SHARED), F32),
        ),
        in_specs=[placed] * 3,
        out_specs=(placed, whole),
        scratch_shapes=[
            vmem(2, 2, 64, ORDER), pltpu.VMEM((8, ORDER), jnp.int32), pltpu.VMEM((8, ORDER), jnp.int32),
            vmem(2, 64, ORDER),
            vmem(2, RING, 2, 32, 512), vmem(2, RING, 2, 32, 512), vmem(2, 2, 32, 512), vmem(2, 2, 32, 512),
            vmem(2, RING, 2, 32, 512), vmem(2, RING, 2, 32, 256), vmem(2, 2, 32, 512), vmem(2, 2, 32, 256),
            vmem(2, 32, 512), vmem(2, 32, 512), vmem(2, 32, 512), vmem(2, 32, 512),
            vmem(2, 32, 256), vmem(2, 32, 256),
            vmem(512, 1024, dtype=BF16), vmem(4, 128, 256, dtype=BF16),
            vmem(512, 1024, dtype=BF16), vmem(4, 128, 256, dtype=BF16),
            vmem(2, 2, 2, 512, 512, dtype=BF16),
            vmem(2, 2, 2, 512, 512, dtype=BF16),
            vmem(2, 2, 2, 512, 256, dtype=BF16),
            pltpu.SemaphoreType.DMA((TOTAL,)),
            pltpu.SemaphoreType.DMA((TOTAL,)),
            pltpu.SemaphoreType.DMA((5,)),
        ],
        compiler_params=pltpu.CompilerParams(
            collective_id=0, has_side_effects=True, vmem_limit_bytes=58 * 1024 * 1024
        ),
    )(child_maps, child_faces, parent_faces)


def solution(mesh):
    placed = (P(None, "box", "row", None), P(), P())
    return jax.shard_map(
        per_device,
        mesh=mesh,
        in_specs=placed,
        out_specs=(P(None, "box", "row", None), P(None, "row", "box")),
        check_vma=False,
    )
```

profile of v0, /device:TPU:1, one launch (start us, length us, event | category | flops | bytes accessed | tf_op | source)
XLA Modules:
  0.0 98.5 jit_solution(3543616376734884946)
XLA Ops:
  0.6 95.2 %shard_map.50 = (f32[2,1,64,1024]{3,2,1,0:T(8,128)}, f32[2,64,512]{2,1,0:T(8,128)}) custom-call(f32[2,2,64,1024]{3,2,1,0:T(8,128)} %maps_ref.1, s32[32,1024]{1,0:T(8,128)} %child_faces_ref.1, s32[16,1024]{1,0:T(8,128)} %parent_faces_ref.1), custom_call_target="tpu_custom_call" | custom-call | tf_op jit(solution)/shard_map/pallas_call | solution.py:469
  95.8 0.0 copy-start
  95.8 1.9 %copy.7 = f32[2,1,64,1024]{3,2,1,0:T(8,128)} copy(f32[2,1,64,1024]{3,2,1,0:T(8,128)} %get-tuple-element.4) | data formatting | bytes 1048576
  97.8 0.0 copy-done
  97.8 0.7 copy.8
Async XLA Ops:
  95.8 1.9 %copy-start = (f32[2,64,512]{2,1,0:T(8,128)S(1)}, f32[2,64,512]{2,1,0:T(8,128)}, u32[]{:S(2)}) copy-start(f32[2,64,512]{2,1,0:T(8,128)} %get-tuple-element.5) | copy-start | bytes 786436
where the time goes:
time: 98.6 us; the launch traced here: 98.5 us
  Pallas kernels  95.2 us (97%)
  local copies, waits for them, and re-layouts  2.63 us (3%)
    pallas_call x1, Pallas kernels, per_device(): pl.pallas_call(kernel, out_shape=(jax.ShapeDtypeStruct((2, 1, 64, ORDER),...  95.2 us
    unnamed x4, local copies, waits for them, and re-layouts  2.63 us

commit v1 on v0

v1 whole, which is shorter than its diff:
```python
import functools

import jax
import jax.numpy as jnp
from jax import lax
from jax.experimental import pallas as pl
from jax.experimental.pallas import tpu as pltpu
from jax.sharding import PartitionSpec as P

MESH = pl.DeviceIdType.MESH
F32 = jnp.float32
BF16 = jnp.bfloat16
ORDER = 1024
SHARED = 512
RING = 16
TOTAL = 208
DEPTHS = (4, 4)


def order_parent(ssm, sso, xa, mb, ob):
    return [
        (ssm, 0), (mb, 0), (sso, 0), (ssm, 1), (xa, 0), (sso, 1), (ssm, 2), (sso, 2), (xa, 1),
        (ssm, 3), (sso, 3), (ob, 0), (mb, 1), (xa, 2), (ob, 1), (mb, 2), (xa, 3), (ob, 2),
        (mb, 3), (ob, 3),
    ]


def order_grand(ssi, ssr, sso, sxm, sxo):
    return [
        (ssi, 0), (ssr, 0), (sso, 0), (ssi, 1), (ssr, 1), (sso, 1), (sxm, 2), (ssi, 2), (ssr, 2),
        (sso, 2), (sxo, 0), (ssi, 3), (ssr, 3), (sso, 3), (sxo, 1), (sxm, 3), (sxo, 2), (sxo, 3),
    ]


def dot(a, b):
    return jnp.dot(a, b, preferred_element_type=F32)


def dot_nt(a, b):
    return lax.dot_general(a, b, (((1,), (1,)), ((), ())), preferred_element_type=F32)


def split(x):
    hi = x.astype(BF16)
    return hi, (x - hi.astype(F32)).astype(BF16)


def iota(shape, dim):
    return lax.broadcasted_iota(jnp.int32, shape, dim)


def one_hot(mask):
    return jnp.where(mask, 1.0, 0.0).astype(BF16)


def prefix_counts(rows):
    width = rows.shape[1]
    lower = one_hot(iota((width, width), 0) < iota((width, width), 1))
    return dot(jnp.where(rows < 0, 1.0, 0.0).astype(BF16), lower).astype(jnp.int32)


def chunked(faces):
    return jnp.concatenate([faces[:, 256 * t : 256 * t + 256] for t in range(4)], axis=0)


def build_selectors(own, other, local, face_ref, outer_ref):
    rows = jnp.concatenate([chunked(own), chunked(other)], axis=0)
    counts = prefix_counts(rows)
    lane = iota((1, 256), 1)
    slot = iota((128, 256), 0)
    own_value = own.astype(F32)
    for t in range(4):
        outer_rank = jnp.where(rows[t : t + 1] < 0, counts[t : t + 1], -1)
        outer_ref[t] = one_hot(outer_rank == slot)
        face_row = rows[4 + t : 5 + t]
        shared_rank = jnp.where(face_row < 0, -1, lane - counts[4 + t : 5 + t])
        wanted = jnp.sum(
            jnp.where(shared_rank == slot, face_row.astype(F32), 0.0), axis=1, keepdims=True
        )
        face_ref[128 * t : 128 * t + 128, :] = one_hot(own_value == wanted)
    count = prefix_counts(jnp.broadcast_to(local, (8, 64)))[0:1]
    target = jnp.where(local < 0, 32 + count, iota((1, 64), 1) - count)
    return one_hot(target == iota((64, 64), 0))


def select_rows(parts, row_hot):
    stack = []
    for value in parts:
        for piece in split(value):
            stack.append(dot(row_hot, piece).astype(BF16))
    return jnp.concatenate(stack, axis=0)


def joined(stack):
    return [stack[0:64] + stack[64:128], stack[128:192] + stack[192:256]]


def pick(par, former, latter):
    return jnp.where(par == 0, former, latter)


def complex_product(x, w):
    m = x[0].shape[0]
    hi, lo = split(jnp.concatenate(x, axis=0))
    both = jnp.concatenate([hi, lo], axis=0)
    sums = []
    for part in range(2):
        main = dot(both, w[0, part])
        sums.append(main[: 2 * m] + main[2 * m :] + dot(hi, w[1, part]))
    by_real, by_imag = sums
    return [by_real[:m] - by_imag[m:], by_imag[:m] + by_real[m:]]


def convert(fetch, pieces):
    @pl.loop(0, RING)
    def _(k):
        rows = pl.ds(pl.multiple_of(k * 32, 32), 32)
        for part in range(2):
            hi, lo = split(fetch(k, part))
            pieces[0, part, rows, :] = hi
            pieces[1, part, rows, :] = lo


def weave(alpha, beta):
    return jnp.concatenate([alpha[0:16], beta[0:16], alpha[16:32], beta[16:32]], axis=0)


def kernel(
    maps_ref, child_faces_ref, parent_faces_ref, parent_out, grand_ref,
    maps, child_rows, parent_rows, parent_ref,
    ss1, sx1a, sx1b, xs1, xx1, ss2, sx2, xs2, xx2, out_ss, out_sx, out_xs, out_xx, out_sx2, out_xx2,
    face_hot, outer_hot, face_hot2, outer_hot2, place_hot, wss, wsx, wsx2, send, recv, local_sem,
):
    box, row = lax.axis_index("box"), lax.axis_index("row")
    par = lax.rem(box, 2)
    mate = box + 1 - 2 * par
    core = lax.rem(row, 2)
    z = lax.div(row, 2)
    sib = row + 1 - 2 * core
    up, down = lax.rem(row + 2, RING), lax.rem(row + RING - 2, RING)
    to_up, to_down, to_sib, to_mate = (box, up), (box, down), (box, sib), (mate, row)

    barrier = pltpu.get_barrier_semaphore()
    for target in (to_up, to_down, to_sib, to_mate):
        pl.semaphore_signal(barrier, inc=1, device_id=target, device_id_type=MESH)

    first = 2 * (box - par)

    def group(i):
        return pl.ds(pl.multiple_of(8 * lax.div(i, 8), 8), 8)

    loads = [
        pltpu.make_async_copy(child_faces_ref.at[group(first)], child_rows, local_sem.at[0]),
        pltpu.make_async_copy(maps_ref.at[:, 1 - par], maps.at[1], local_sem.at[1]),
        pltpu.make_async_copy(maps_ref.at[:, par], maps.at[0], local_sem.at[2]),
        pltpu.make_async_copy(parent_faces_ref.at[group(box)], parent_rows, local_sem.at[3]),
    ]
    for c in loads:
        c.start()

    ids = {}
    pending = []

    def copy(src, dst, target, key):
        k = ids.setdefault(key, len(ids))
        return pltpu.make_async_remote_copy(
            src_ref=src, dst_ref=dst, send_sem=send.at[k], recv_sem=recv.at[k],
            device_id=target, device_id_type=MESH,
        )

    def push(src, dst, target, key):
        c = copy(src, dst, target, key)
        c.start()
        pending.append(c)

    def drain(spare):
        while len(pending) > spare:
            pending.pop(0).wait_send()

    def arrived(dst, key):
        copy(dst, dst, to_mate, key).wait_recv()

    def away(base, way, hops):
        return lax.rem(base + 2 * RING + (2 if way else -2) * hops, RING)

    class Section:
        settled = -1

        def __init__(self, name, buf, part=None, forward=False, source=None):
            self.name, self.buf, self.part, self.forward, self.source = name, buf, part, forward, source

        def block(self, slot):
            return self.buf.at[slot] if self.part is None else self.buf.at[slot, self.part]

        def piece(self, base, way, hop):
            slot = away(base, way, hop)
            if hop < 3:
                return self.block(slot)
            if self.part is not None:
                return self.buf.at[slot, self.part, pl.ds(16 * way, 16)]
            return self.buf.at[slot, way]

        def to_mate(self, slot, what):
            if self.forward:
                block = self.block(slot)
                push(block, block, to_mate, (self.name, "mate", what))

        def send(self, way, hop):
            if hop == 0 and way == 0 and self.source is not None:
                arrived(*self.source)
            piece = self.piece(row, way, hop)
            push(piece, piece, to_down if way else to_up, (self.name, way, hop))
            if hop == 0 and way == 1:
                own = self.block(row)
                push(own, own, to_sib, (self.name, "sib", "own"))
                self.to_mate(row, "own")

        def receive(self, way, hop):
            slot = away(row, way, hop + 1)
            if hop < 3:
                piece = self.block(slot)
            else:
                piece = self.piece(away(row, way, 1), way, hop)
            arrived(piece, (self.name, way, hop))
            return slot, piece

        def share(self, way, hop, slot, piece):
            push(piece, piece, to_sib, (self.name, "sib", way, hop))
            if hop < 3:
                self.to_mate(slot, (way, hop))
            elif way == 1:
                self.to_mate(slot, "far")

        def settle(self, hop):
            while self.settled <= hop:
                if self.settled < 0:
                    arrived(self.block(sib), (self.name, "sib", "own"))
                else:
                    for way in range(2):
                        if self.settled < 3:
                            piece = self.block(away(sib, way, self.settled + 1))
                        else:
                            piece = self.piece(away(sib, way, 1), way, 3)
                        arrived(piece, (self.name, "sib", way, self.settled))
                self.settled += 1

        def done(self):
            self.settle(3)

    class Flow:
        def __init__(self, order, depth):
            self.order, self.depth = order, depth
            self.sent = self.got = 0

        def ready(self, got):
            more = []
            while self.sent < len(self.order) and self.sent < got + self.depth:
                section, hop = self.order[self.sent]
                if hop and (section, hop - 1) not in self.order[:got]:
                    break
                more.append((section, hop))
                self.sent += 1
            return more

        def begin(self):
            for section, hop in self.ready(self.got):
                for way in range(2):
                    section.send(way, hop)

        def extend(self, order):
            self.order += order
            self.begin()

        def advance(self, upto=None):
            upto = self.got + 1 if upto is None else upto
            while self.got < min(upto, len(self.order)):
                section, hop = self.order[self.got]
                following = self.ready(self.got + 1)
                now = [pair for pair in following if pair[1]]
                shared = []
                for way in range(2):
                    shared.append((way, hop, *section.receive(way, hop)))
                    for later, later_hop in now:
                        later.send(way, later_hop)
                for one in shared:
                    section.share(*one)
                for later, later_hop in following:
                    for way in range(2):
                        if not later_hop:
                            later.send(way, later_hop)
                section.settle(hop - 1)
                self.got += 1

        def through(self, section):
            return self.order.index((section, 3)) + 1

    class Mirror:
        def __init__(self, name, mine, buf):
            self.name, self.mine, self.buf = name, mine, buf

        def block(self, slot):
            return self.buf.at[slot, 1]

        def take(self, slot, what):
            block = self.block(slot)
            arrived(block, (self.mine, "mate", what))
            push(block, block, to_sib, (self.name, "sib", what))

        def start(self):
            self.take(row, "own")

        def step(self, j):
            for way in range(2):
                self.take(away(row, way, j + 1), (way, j))
            self.settle(j - 1)

        def last(self):
            self.take(away(row, 0, 4), "far")
            self.settle(2)

        def settle(self, j):
            if j < 0:
                arrived(self.block(sib), (self.name, "sib", "own"))
            else:
                for way in range(2):
                    arrived(self.block(away(sib, way, j + 1)), (self.name, "sib", (way, j)))

        def done(self):
            arrived(self.block(away(sib, 0, 4)), (self.name, "sib", "far"))

    def faces_of(rows, i):
        inside = lax.rem(i, 8)
        lanes = pl.ds(pl.multiple_of(z * 128, 128), 128)
        whole = jnp.sum(
            jnp.where(iota((8, ORDER), 0) == inside, rows[...], 0), axis=0, keepdims=True
        )
        chunk = jnp.sum(
            jnp.where(iota((8, 128), 0) == inside, rows[:, lanes], 0), axis=0, keepdims=True
        )
        local = jnp.where(core == 0, chunk[:, :64], chunk[:, 64:])
        return whole, local

    def select(child, own_index, pair_index):
        own_faces, local = faces_of(child_rows, own_index)
        paired, _ = faces_of(child_rows, pair_index)
        hot = build_selectors(own_faces, paired, local, face_hot, outer_hot)
        loads[2 - child].wait()
        stack = select_rows([maps[child, part] for part in range(2)], hot)
        face = joined(dot_nt(stack, face_hot[...]))
        outer = jnp.concatenate(
            [dot_nt(stack[:, 256 * t : 256 * t + 256], outer_hot[t]) for t in range(4)], axis=1
        )
        return face, joined(outer)

    loads[0].wait()
    face, outer = select(1, first + 1 + par, first + 3 - 3 * par)
    for part in range(2):
        out_ss[part] = face[part][:32]
        out_xs[part] = face[part][32:]
        out_xx[part] = outer[part][32:]
        halves = [outer[part][:32, :256], outer[part][:32, 256:]]
        out_sx[0, part] = pick(par, halves[1], halves[0])
        out_sx[1, part] = pick(par, halves[0], halves[1])
    pl.semaphore_wait(barrier, 4)
    push(out_ss, ss1.at[par, row], to_mate, "ss1")

    face, outer = select(0, first + 3 * par, first + 2 - par)
    for part in range(2):
        ss1[par, row, part] = face[part][:32]
        xs1[par, part] = face[part][32:]
        xx1[par, part] = outer[part][32:]
        halves = [outer[part][:32, :256], outer[part][:32, 256:]]
        sx1a[row, par, part] = pick(par, halves[0], halves[1])
        sx1b[par, row, part] = pick(par, halves[1], halves[0])
    ssm = Section("ssm1", ss1.at[par])
    sso = Section("sso1", ss1.at[1 - par], source=(ss1.at[1 - par, row], "ss1"))
    xa = Section("sxa1", sx1a, source=(sx1a.at[row, 1 - par], "mate sxa1"))
    mb = Section("sxm1", sx1b.at[par])
    ob = Section("sxo1", sx1b.at[1 - par], source=(sx1b.at[1 - par, row], "mate sxb1"))
    flow = Flow(order_parent(ssm, sso, xa, mb, ob), 2)
    flow.begin()
    push(out_sx.at[0], sx1a.at[row, par], to_mate, "mate sxa1")
    flow.depth = DEPTHS[0]
    flow.begin()

    def horner(ss, xs, more):
        convert(lambda k, part: ss[1, k, part], wss.at[1])
        u = [xs[0, part] for part in range(2)]
        lead = complex_product(u, wss.at[1])
        base = [jnp.concatenate([lead[part], -xs[1, part]], axis=0) for part in range(2)]
        more()
        convert(lambda k, part: ss[0, k, part], wss.at[0])
        w = base
        for term in range(3):
            t = complex_product(w, wss.at[0])
            more()
            t = complex_product(t, wss.at[1])
            w = [base[part] + t[part] for part in range(2)]
            more()
        t = complex_product(w, wss.at[0])
        t = [jnp.concatenate([t[part][:32] + u[part], t[part][32:]], axis=0) for part in range(2)]
        return w, t

    rank, place = iota((256, 256), 0), iota((256, 256), 1)
    inside = jnp.where(rank < 128, rank, rank - 128)
    spot = 32 * lax.div(inside, 16) + lax.rem(inside, 16) + jnp.where(rank < 128, 0, 16)
    place_hot[...] = one_hot(spot == place)

    def finish(w, t, wx, xx):
        alpha, beta = complex_product(w, wx.at[0]), complex_product(t, wx.at[1])
        tiles = []
        for part in range(2):
            left = weave(xx[0][part] + alpha[part][:32], alpha[part][32:])
            right = weave(-beta[part][:32], xx[1][part] - beta[part][32:])
            tiles.append((left, right))
        columns = []
        for tile in range(2):
            cols = slice(128 * tile, 128 * tile + 128)
            packed = jnp.concatenate(
                [jnp.concatenate([left[:, cols], right[:, cols]], axis=1) for left, right in tiles],
                axis=0,
            )
            hi, lo = split(packed)
            spread = dot(jnp.concatenate([hi, lo], axis=0), place_hot[...])
            columns.append(spread[:128] + spread[128:])
        both = jnp.concatenate(columns, axis=1)
        return [both[:64], both[64:]]

    loads[3].wait()
    own, loc = faces_of(parent_rows, box)
    pair, _ = faces_of(parent_rows, mate)
    hot2 = build_selectors(own, pair, loc, face_hot2, outer_hot2)
    flow.advance(2)
    push(out_sx.at[1], sx1b.at[par, row], to_mate, "mate sxb1")
    flow.advance(3)
    push(out_xs, xs1.at[par], to_mate, "xs1")
    push(out_xx, xx1.at[par], to_mate, "xx1")
    flow.advance(max(flow.through(ssm), flow.through(sso)))
    arrived(xs1.at[1 - par], "xs1")
    arrived(xx1.at[1 - par], "xx1")
    ssm.done()
    sso.done()
    w, t = horner(ss1, xs1, lambda: flow.advance(min(flow.got + 1, flow.through(xa))))

    ssi, ssr = Section("ssi2", ss2.at[par], part=1, forward=True), Section("ssr2", ss2.at[par], part=0)
    sso = Section("sso2", ss2.at[1 - par], part=0, source=(ss2.at[1 - par, row, 0], "ss2"))
    mirror = Mirror("mir2", "ssi2", ss2.at[1 - par])
    sxm = Section("sxm2", sx2.at[par])
    sxo = Section("sxo2", sx2.at[1 - par], source=(sx2.at[1 - par, row], "sx2"))
    face = jnp.zeros((256, 512), F32)
    for h in range(2):
        side = par if h == 0 else 1 - par
        lanes = pl.ds(pl.multiple_of(256 * side, 256), 256)
        if h == 0:
            flow.advance(flow.through(xa))
            xa.done()
        else:
            flow.advance(max(flow.through(mb), flow.through(ob)) + 1)
            mb.done()
            ob.done()
        for role in range(2):
            if h == 0:
                convert(lambda k, part: sx1a[k, role, part], wsx.at[h, role])
            else:
                convert(lambda k, part: sx1b[role, k, part], wsx.at[h, role])
        xx = [[xx1[role, part, :, lanes] for part in range(2)] for role in range(2)]
        merged = finish(w, t, wsx.at[h], xx)
        wide = pl.ds(pl.multiple_of(512 * side, 512), 512)
        for part in range(2):
            parent_ref[part, :, wide] = merged[part]
        stack = select_rows(merged, hot2)
        outer = joined(
            jnp.concatenate(
                [dot_nt(stack[:, 256 * i : 256 * i + 256], outer_hot2[2 * side + i]) for i in range(2)],
                axis=1,
            )
        )
        if h == 0:
            for part in range(2):
                sx2[par, row, part] = outer[part][:32]
                xx2[par, part] = outer[part][32:]
            flow.extend([(sxm, 0), (sxm, 1)])
        face = face + dot_nt(stack, face_hot2[:, wide])
    face = joined(face)
    for part in range(2):
        ss2[par, row, part] = face[part][:32]
        xs2[par, part] = face[part][32:]
    real = ss2.at[par, row, 0]
    push(real, real, to_mate, "ss2")
    flow.depth = DEPTHS[1]
    flow.extend(order_grand(ssi, ssr, sso, sxm, sxo))
    for part in range(2):
        out_sx2[part] = outer[part][:32]
        out_xx2[part] = outer[part][32:]
    push(out_sx2, sx2.at[par, row], to_mate, "sx2")
    store = pltpu.make_async_copy(parent_ref, parent_out.at[:, 0], local_sem.at[4])
    store.start()
    drain(30)
    at = [flow.order.index((ssi, hop)) + 1 for hop in range(4)]
    flow.advance(at[0])
    push(xs2.at[par], xs2.at[par], to_mate, "xs2")
    mirror.start()
    flow.advance(at[1])
    mirror.step(0)
    push(out_xx2, xx2.at[par], to_mate, "xx2")
    flow.advance(at[2])
    mirror.step(1)
    flow.advance(max(flow.through(ssi), flow.through(ssr), flow.through(sso)))
    mirror.step(2)
    mirror.last()
    arrived(xs2.at[1 - par], "xs2")
    arrived(xx2.at[1 - par], "xx2")
    flow.advance()
    ssi.done()
    ssr.done()
    sso.done()
    mirror.done()
    w, t = horner(ss2, xs2, flow.advance)
    drain(16)
    flow.advance(len(flow.order))
    sxm.done()
    sxo.done()
    for role in range(2):
        convert(lambda k, part: sx2[role, k, part], wsx2.at[role])
    xx = [[xx2[role, part] for part in range(2)] for role in range(2)]
    merged = finish(w, t, wsx2, xx)
    for part in range(2):
        grand_ref[part] = merged[part]

    store.wait()
    drain(0)
    assert len(ids) <= TOTAL


def per_device(child_maps, child_faces, parent_faces):
    def vmem(*shape, dtype=F32):
        return pltpu.VMEM(shape, dtype)

    whole = pl.BlockSpec(memory_space=pltpu.VMEM)
    placed = pl.BlockSpec(memory_space=pltpu.HBM)
    return pl.pallas_call(
        kernel,
        out_shape=(
            jax.ShapeDtypeStruct((2, 1, 64, ORDER), F32),
            jax.ShapeDtypeStruct((2, 64, SHARED), F32),
        ),
        in_specs=[placed] * 3,
        out_specs=(placed, whole),
        scratch_shapes=[
            vmem(2, 2, 64, ORDER), pltpu.VMEM((8, ORDER), jnp.int32), pltpu.VMEM((8, ORDER), jnp.int32),
            vmem(2, 64, ORDER),
            vmem(2, RING, 2, 32, 512), vmem(RING, 2, 2, 32, 256), vmem(2, RING, 2, 32, 256), vmem(2, 2, 32, 512), vmem(2, 2, 32, 512),
            vmem(2, RING, 2, 32, 512), vmem(2, RING, 2, 32, 256), vmem(2, 2, 32, 512), vmem(2, 2, 32, 256),
            vmem(2, 32, 512), vmem(2, 2, 32, 256), vmem(2, 32, 512), vmem(2, 32, 512),
            vmem(2, 32, 256), vmem(2, 32, 256),
            vmem(512, 1024, dtype=BF16), vmem(4, 128, 256, dtype=BF16),
            vmem(512, 1024, dtype=BF16), vmem(4, 128, 256, dtype=BF16),
            vmem(256, 256, dtype=BF16),
            vmem(2, 2, 2, 512, 512, dtype=BF16),
            vmem(2, 2, 2, 2, 512, 256, dtype=BF16),
            vmem(2, 2, 2, 512, 256, dtype=BF16),
            pltpu.SemaphoreType.DMA((TOTAL,)),
            pltpu.SemaphoreType.DMA((TOTAL,)),
            pltpu.SemaphoreType.DMA((5,)),
        ],
        compiler_params=pltpu.CompilerParams(
            collective_id=0, has_side_effects=True, vmem_limit_bytes=58 * 1024 * 1024
        ),
    )(child_maps, child_faces, parent_faces)


def solution(mesh):
    placed = (P(None, "box", "row", None), P(), P())
    return jax.shard_map(
        per_device,
        mesh=mesh,
        in_specs=placed,
        out_specs=(P(None, "box", "row", None), P(None, "row", "box")),
        check_vma=False,
    )
```

time: 98.6 us -> 97.7 us (level)
  no operation moved by 1% of the time
where the time goes in v1:
time: 97.7 us; the launch traced here: 97.6 us
  Pallas kernels  94.3 us (97%)
  local copies, waits for them, and re-layouts  2.63 us (3%)
    pallas_call x1, Pallas kernels, per_device(): pl.pallas_call(kernel, out_shape=(jax.ShapeDtypeStruct((2, 1, 64, ORDER),...  94.3 us
    unnamed x4, local copies, waits for them, and re-layouts  2.63 us

profile of v1, /device:TPU:1, one launch (start us, length us, event | category | flops | bytes accessed | tf_op | source)
XLA Modules:
  0.0 97.6 jit_solution(1519464078869706201)
XLA Ops:
  0.6 94.3 %shard_map.50 = (f32[2,1,64,1024]{3,2,1,0:T(8,128)}, f32[2,64,512]{2,1,0:T(8,128)}) custom-call(f32[2,2,64,1024]{3,2,1,0:T(8,128)} %maps_ref.1, s32[32,1024]{1,0:T(8,128)} %child_faces_ref.1, s32[16,1024]{1,0:T(8,128)} %parent_faces_ref.1), custom_call_target="tpu_custom_call" | custom-call | tf_op jit(solution)/shard_map/pallas_call | solution.py:541
  94.9 0.0 copy-start
  94.9 1.9 %copy.7 = f32[2,1,64,1024]{3,2,1,0:T(8,128)} copy(f32[2,1,64,1024]{3,2,1,0:T(8,128)} %get-tuple-element.4) | data formatting | bytes 1048576
  96.8 0.0 copy-done
  96.8 0.7 copy.8
Async XLA Ops:
  94.9 1.9 %copy-start = (f32[2,64,512]{2,1,0:T(8,128)S(1)}, f32[2,64,512]{2,1,0:T(8,128)}, u32[]{:S(2)}) copy-start(f32[2,64,512]{2,1,0:T(8,128)} %get-tuple-element.5) | copy-start | bytes 786436

commit v2 on v1

--- a/solution.py
+++ b/solution.py
@@ -406,8 +406,7 @@
     spot = 32 * lax.div(inside, 16) + lax.rem(inside, 16) + jnp.where(rank < 128, 0, 16)
     place_hot[...] = one_hot(spot == place)
 
-    def finish(w, t, wx, xx):
-        alpha, beta = complex_product(w, wx.at[0]), complex_product(t, wx.at[1])
+    def finish(alpha, beta, xx):
         tiles = []
         for part in range(2):
             left = weave(xx[0][part] + alpha[part][:32], alpha[part][32:])
@@ -464,7 +463,8 @@
             else:
                 convert(lambda k, part: sx1b[role, k, part], wsx.at[h, role])
         xx = [[xx1[role, part, :, lanes] for part in range(2)] for role in range(2)]
-        merged = finish(w, t, wsx.at[h], xx)
+        alpha, beta = complex_product(w, wsx.at[h, 0]), complex_product(t, wsx.at[h, 1])
+        merged = finish(alpha, beta, xx)
         wide = pl.ds(pl.multiple_of(512 * side, 512), 512)
         for part in range(2):
             parent_ref[part, :, wide] = merged[part]
@@ -517,13 +517,18 @@
     mirror.done()
     w, t = horner(ss2, xs2, flow.advance)
     drain(16)
-    flow.advance(len(flow.order))
-    sxm.done()
-    sxo.done()
-    for role in range(2):
+    products = []
+    for section, role, rows in ((sxm, par, (w, t)), (sxo, 1 - par, (t, w))):
+        flow.advance(flow.through(section))
+        section.done()
         convert(lambda k, part: sx2[role, k, part], wsx2.at[role])
+        picked = [pick(par, rows[0][part], rows[1][part]) for part in range(2)]
+        products.append(complex_product(picked, wsx2.at[role]))
+    own, far = products
+    alpha = [pick(par, own[part], far[part]) for part in range(2)]
+    beta = [pick(par, far[part], own[part]) for part in range(2)]
     xx = [[xx2[role, part] for part in range(2)] for role in range(2)]
-    merged = finish(w, t, wsx2, xx)
+    merged = finish(alpha, beta, xx)
     for part in range(2):
         grand_ref[part] = merged[part]
 

time: 97.7 us -> 98.3 us (level)
  no operation moved by 1% of the time
where the time goes in v2:
time: 98.3 us; the launch traced here: 98.2 us
  Pallas kernels  94.9 us (97%)
  local copies, waits for them, and re-layouts  2.63 us (3%)
    pallas_call x1, Pallas kernels, per_device(): pl.pallas_call(kernel, out_shape=(jax.ShapeDtypeStruct((2, 1, 64, ORDER),...  94.9 us
    unnamed x4, local copies, waits for them, and re-layouts  2.63 us

profile of v2, /device:TPU:1, one launch (start us, length us, event | category | flops | bytes accessed | tf_op | source)
XLA Modules:
  0.0 98.2 jit_solution(100843906374705595)
XLA Ops:
  0.6 94.9 %shard_map.50 = (f32[2,1,64,1024]{3,2,1,0:T(8,128)}, f32[2,64,512]{2,1,0:T(8,128)}) custom-call(f32[2,2,64,1024]{3,2,1,0:T(8,128)} %maps_ref.1, s32[32,1024]{1,0:T(8,128)} %child_faces_ref.1, s32[16,1024]{1,0:T(8,128)} %parent_faces_ref.1), custom_call_target="tpu_custom_call" | custom-call | tf_op jit(solution)/shard_map/pallas_call | solution.py:546
  95.5 0.0 copy-start
  95.5 1.9 %copy.7 = f32[2,1,64,1024]{3,2,1,0:T(8,128)} copy(f32[2,1,64,1024]{3,2,1,0:T(8,128)} %get-tuple-element.4) | data formatting | bytes 1048576
  97.5 0.0 copy-done
  97.5 0.7 copy.8
Async XLA Ops:
  95.5 1.9 %copy-start = (f32[2,64,512]{2,1,0:T(8,128)S(1)}, f32[2,64,512]{2,1,0:T(8,128)}, u32[]{:S(2)}) copy-start(f32[2,64,512]{2,1,0:T(8,128)} %get-tuple-element.5) | copy-start | bytes 786436

commit v3 on v1

--- a/solution.py
+++ b/solution.py
@@ -126,7 +126,7 @@
 
 
 def kernel(
-    maps_ref, child_faces_ref, parent_faces_ref, parent_out, grand_ref,
+    maps_ref, faces_ref, parent_out, grand_ref,
     maps, child_rows, parent_rows, parent_ref,
     ss1, sx1a, sx1b, xs1, xx1, ss2, sx2, xs2, xx2, out_ss, out_sx, out_xs, out_xx, out_sx2, out_xx2,
     face_hot, outer_hot, face_hot2, outer_hot2, place_hot, wss, wsx, wsx2, send, recv, local_sem,
@@ -150,10 +150,10 @@
         return pl.ds(pl.multiple_of(8 * lax.div(i, 8), 8), 8)
 
     loads = [
-        pltpu.make_async_copy(child_faces_ref.at[group(first)], child_rows, local_sem.at[0]),
+        pltpu.make_async_copy(faces_ref.at[group(first)], child_rows, local_sem.at[0]),
         pltpu.make_async_copy(maps_ref.at[:, 1 - par], maps.at[1], local_sem.at[1]),
         pltpu.make_async_copy(maps_ref.at[:, par], maps.at[0], local_sem.at[2]),
-        pltpu.make_async_copy(parent_faces_ref.at[group(box)], parent_rows, local_sem.at[3]),
+        pltpu.make_async_copy(faces_ref.at[group(32 + box)], parent_rows, local_sem.at[3]),
     ]
     for c in loads:
         c.start()
@@ -544,7 +544,7 @@
             jax.ShapeDtypeStruct((2, 1, 64, ORDER), F32),
             jax.ShapeDtypeStruct((2, 64, SHARED), F32),
         ),
-        in_specs=[placed] * 3,
+        in_specs=[placed] * 2,
         out_specs=(placed, whole),
         scratch_shapes=[
             vmem(2, 2, 64, ORDER), pltpu.VMEM((8, ORDER), jnp.int32), pltpu.VMEM((8, ORDER), jnp.int32),
@@ -564,9 +564,9 @@
             pltpu.SemaphoreType.DMA((5,)),
         ],
         compiler_params=pltpu.CompilerParams(
-            collective_id=0, has_side_effects=True, vmem_limit_bytes=58 * 1024 * 1024
+            collective_id=0, has_side_effects=True, vmem_limit_bytes=54000 * 1024
         ),
-    )(child_maps, child_faces, parent_faces)
+    )(child_maps, jnp.concatenate([child_faces, parent_faces], axis=0))
 
 
 def solution(mesh):

time: 97.7 us -> 96.7 us (0.990)
  local copies, waits for them, and re-layouts: 2.63 us -> 1.5 us
    unnamed x4 -> x2, local copies, waits for them, and re-layouts: 2.63 us -> 1.5 us
where the time goes in v3:
time: 96.7 us; the launch traced here: 96.6 us
  Pallas kernels  93.5 us (97%)
  local copies, waits for them, and re-layouts  1.5 us (2%)
    pallas_call x1, Pallas kernels, per_device(): pl.pallas_call(kernel, out_shape=(jax.ShapeDtypeStruct((2, 1, 64, ORDER),...  93.5 us

profile of v3, /device:TPU:1, one launch (start us, length us, event | category | flops | bytes accessed | tf_op | source)
XLA Modules:
  0.0 96.6 jit_solution(8888100344506816893)
XLA Ops:
  0.6 1.0 pad_add_fusion.faces_ref
  1.6 93.5 %shard_map.50 = (f32[2,1,64,1024]{3,2,1,0:T(8,128)S(1)}, f32[2,64,512]{2,1,0:T(8,128)S(1)}) custom-call(f32[2,2,64,1024]{3,2,1,0:T(8,128)} %maps_ref.1, s32[48,1024]{1,0:T(8,128)S(1)} %pad_add_fusion.faces_ref), custom_call_target="tpu_custom_call" | custom-call | tf_op jit(solution)/shard_map/pallas_call | solution.py:541
  95.1 0.8 copy.7
  95.9 0.7 copy.8
